TPU v7x, 128 devices: a whole 4x4x4 slice. The times are simulated.
128 devices in a mesh: tile: 16 (over y_lo, z, core), member: 8 (over y_hi, x).
Axes of the slice: x: 4, y: 4 (y_hi: 2, y_lo: 2; y = y_hi * 2 + y_lo), z: 4, core: 2. Of those that a mesh axis runs over, the one named last changes fastest.
Arguments:
- coeffs: float32 [80, 32, 16384], P('member', None, 'tile'), may hold values from -6 to 6
- perturb: bfloat16 [2, 80, 32, 16384], P(None, 'member', None, 'tile'), may hold values from -1.25 to 1.25
- blocks: bfloat16 [16, 5, 1024, 1024], P('tile'), may hold values from -0.125 to 0.125
- neighbours: int32 [16, 5], P('tile'), may hold values from 0 to 15, as said below
- live: int32 [16], P('tile'), may hold values from 2 to 5, as said below
- obs_count: int32 [16], P('tile'), may hold values from 256 to 1024, as said below
- innovation: float32 [2, 32, 16384], P(None, None, 'tile'), may hold values from -6 to 6
- obs_weight: float32 [32, 16384], P(None, 'tile'), may hold values from 0.25 to 4
Outputs:
- increment: float32 [2, 32, 16384], P(None, None, ('tile', 'member'))
- gradient: float32 [80, 32, 16384], P('member', None, 'tile')
Inputs may be any that keep to these rules, and one draw needn't show every extreme that they name: `neighbours`: each row lists 5 different tiles, each at a distance of at most 2 from the row's tile along the tile cycle (indices taken modulo 16); only the first live[i] slots of row i are used. Some tile has all 5 slots live. Observations of tile i lie in its first obs_count[i] columns.
All inputs are finite; a program needn't handle non-finite values.
Results may differ from a plain program's by a relative error of at most 0.0038.
Values may be sent and summed in bfloat16 or wider, within the bound.
A program may use at most 64 MiB of HBM per device.

v0:
```python
import jax
import jax.numpy as jnp
from jax import lax
from jax.sharding import PartitionSpec as P


def shifted(value, axis, steps):
    count = lax.axis_size(axis)
    pairs = [(source, (source + steps) % count) for source in range(count)]
    return lax.ppermute(value, axis, pairs)


def shards(coeffs, perturb, blocks, neighbours, live, obs_count, innovation, obs_weight):
    members, levels, cell_count = coeffs.shape
    row_count = members * levels
    slot_count = blocks.shape[1]
    radius = (slot_count - 1) // 2
    tile_count = lax.axis_size("tile")
    tile_index = lax.axis_index("tile")
    sources = neighbours[0]
    slot_live = jnp.arange(slot_count) < live[0]
    offset = (sources - tile_index) % tile_count
    offset = jnp.where(offset > radius, offset - tile_count, offset)
    coeff_half = coeffs.astype(jnp.bfloat16).reshape(row_count, cell_count)
    nearby = []
    for shift_by in range(-radius, radius + 1):
        if shift_by == 0:
            nearby.append(coeff_half)
        else:
            nearby.append(shifted(coeff_half, "tile", -shift_by))
    pieces = jnp.take(jnp.stack(nearby), offset + radius, axis=0)
    pieces = jnp.where(slot_live[:, None, None], pieces, jnp.zeros_like(pieces))
    localized = jnp.einsum("krc,kcd->rd", pieces, blocks[0], preferred_element_type=jnp.float32)
    localized = localized.reshape(members, levels, cell_count)
    partial_value = jnp.sum(perturb.astype(jnp.float32) * localized[None], axis=1)
    groups = lax.axis_size("member")
    group_index = lax.axis_index("member")
    own_width = cell_count // groups
    summed = lax.psum(partial_value, "member")
    column = jnp.arange(cell_count)
    residual = obs_weight[None] * jnp.where(
        column[None, None, :] < obs_count[0], summed - innovation, 0.0
    )
    increment = lax.dynamic_slice_in_dim(summed, group_index * own_width, own_width, 2)
    adjoint_in = jnp.sum(perturb.astype(jnp.float32) * residual[:, None], axis=0)
    adjoint_in = adjoint_in.astype(jnp.bfloat16).reshape(row_count, cell_count)
    products = jnp.einsum("rd,kcd->krc", adjoint_in, blocks[0], preferred_element_type=jnp.float32)
    products = jnp.where(slot_live[:, None, None], products, jnp.zeros_like(products))
    distances = jnp.arange(2 * radius + 1) - radius
    choose = ((offset[None, :] == distances[:, None]) & slot_live[None, :]).astype(jnp.float32)
    by_offset = jnp.einsum("dk,krc->drc", choose, products, precision=lax.Precision.HIGHEST)
    received = by_offset[radius]
    for shift_by in range(-radius, radius + 1):
        if shift_by != 0:
            received = received + shifted(by_offset[shift_by + radius], "tile", shift_by)
    gradient = coeffs + received.reshape(members, levels, cell_count)
    return (increment, gradient)


def solution(mesh):
    placed = (
        P("member", None, "tile"),
        P(None, "member", None, "tile"),
        P("tile", None, None, None),
        P("tile", None),
        P("tile"),
        P("tile"),
        P(None, None, "tile"),
        P(None, "tile"),
    )
    return jax.shard_map(
        shards,
        mesh=mesh,
        in_specs=placed,
        out_specs=(P(None, None, ("tile", "member")), P("member", None, "tile")),
        check_vma=False,
    )
```

profile of v0, /device:TPU:1, one launch (start us, length us, event | category | flops | bytes accessed | tf_op | source)
XLA Modules:
  0.0 237.3 jit_solution(9589325741751256946)
XLA Ops:
  7.2 1.4 convert_element_type.22
  8.6 5.7 %collective-permute-start.3 = (bf16[320,1024]{1,0:T(8,128)(2,1)S(1)}, bf16[320,1024]{1,0:T(8,128)(2,1)S(1)}, u32[]{:S(2)}, u32[]{:S(2)}) collective-permute-start(bf16[320,1024]{1,0:T(8,128)(2,1)S(1)} %bitcast.79), channel_id=1, source_target_pairs={{0,112},{8,120},{16,0},{24,8},{32,16},{40,24},{48,32},{56,40},{64,... | collective-permute-start | bytes 1966088 | tf_op jit(solution)/shard_map/ppermute | solution.py:10
  14.3 1.0 collective-permute-start.2
  18.7 22.0 %collective-permute-done = bf16[320,1024]{1,0:T(8,128)(2,1)S(1)} collective-permute-done((bf16[320,1024]{1,0:T(8,128)(2,1)S(1)}, bf16[320,1024]{1,0:T(8,128)(2,1)S(1)}, u32[]{:S(2)}, u32[]{:S(2)}) %collective-permute-start) | collective-permute-done | bytes 655392 | tf_op jit(solution)/shard_map/ppermute | solution.py:10
  45.2 2.7 %gather_fusion = bf16[5,320,1024]{2,1,0:T(8,128)(2,1)S(1)} fusion(bf16[5,320,1024]{2,1,0:T(8,128)(2,1)} %bitcast_dynamic-update-slice_fusion, s32[1024]{0:T(1024)S(1)} %pad_clamp_fusion), kind=kCustom, calls=%fused_computation | custom fusion | bytes 6553620 | tf_op jit(solution)/shard_map/jit(_take)/gather | solution.py:31
  48.3 6.6 %fusion.10 = f32[10,32,1024]{2,1,0:T(8,128)S(1)} fusion(bf16[10,32,1024,5]{2,1,0,3:T(8,128)(2,1)S(1)} %bitcast.78, bf16[1,5,1024,1024]{3,2,1,0:T(8,128)(2,1)} %param.10), kind=kOutput, calls=%fused_computation.15 | convolution fusion | flops 3355443200 | bytes 15073280 | tf_op jit(solution)/shard_map/krc,kcd->rd/dot_general | solution.py:33
  55.0 1.0 fusion.8
  56.0 77.1 %all-reduce.2.cloned.1.call-done = f32[2,32,1024]{2,1,0:T(8,128)} async-done(((f32[2,32,1024]{2,1,0:T(8,128)}), f32[2,32,1024]{2,1,0:T(8,128)}) %all-reduce.2.cloned.1.call-update) | async-done | bytes 262160 | tf_op jit(solution)/shard_map/psum | solution.py:39
  133.2 1.0 select_multiply_fusion
  134.5 12.9 %fusion.4 = f32[320,5,1024]{2,0,1:T(8,128)} fusion(bf16[320,1024,1]{1,0,2:T(8,128)(2,1)S(1)} %bitcast.85, bf16[1,5,1024,1024]{3,2,1,0:T(8,128)(2,1)} %param.10), kind=kOutput, calls=%fused_computation.5 | convolution fusion | flops 3355443200 | bytes 17694720 | tf_op jit(solution)/shard_map/rd,kcd->krc/dot_general | solution.py:47
  147.4 13.3 %fusion.2 = f32[5,320,1024]{2,0,1:T(8,128)S(1)} fusion(f32[320,5,1024]{2,0,1:T(8,128)} %fusion.4, pred[5]{0:T(512)(128)(4,1)S(1)} %get-tuple-element.8, s32[5]{0:T(128)S(1)} %fusion.27, s32[5]{0:T(128)S(1)} %iota_add_fusion), kind=kOutput, calls=%fused_computation.3 | convolution fusion | flops 99942448 | bytes 13107245 | tf_op jit(solution)/shard_map/dk,krc->drc/dot_general | solution.py:51
  160.7 6.1 %fusion.29 = (f32[1,320,1024]{2,0,1:T(1,128)}, f32[1,320,1024]{2,0,1:T(1,128)}, f32[1,320,1024]{2,0,1:T(1,128)}, f32[1,320,1024]{2,0,1:T(1,128)}, f32[1,320,1024]{2,0,1:T(1,128)S(1)}) fusion(f32[5,320,1024]{2,0,1:T(8,128)S(1)} %fusion.2), kind=kLoop, calls=%fused_computation.64 | loop fusion | bytes 13107200 | tf_op jit(solution)/shard_map/slice | solution.py:52
  166.8 1.7 copy.45
  168.5 1.3 copy.46
  169.9 1.3 copy.47
  171.2 1.4 copy.44
  172.6 7.3 %collective-permute-start.6 = (f32[320,1024]{1,0:T(8,128)}, f32[320,1024]{1,0:T(8,128)}, u32[]{:S(2)}, u32[]{:S(2)}) collective-permute-start(f32[320,1024]{1,0:T(8,128)} %bitcast.70), channel_id=1, source_target_pairs={{0,8},{8,16},{16,24},{24,32},{32,40},{40,48},{48,56},{56,64},{64,7... | collective-permute-start | bytes 3932168 | tf_op jit(solution)/shard_map/ppermute | solution.py:10
  179.9 1.3 collective-permute-start.7
  181.2 2.3 collective-permute-start.4
  183.5 1.4 constant_dynamic-slice_fusion
  184.9 23.4 %collective-permute-done.6 = f32[320,1024]{1,0:T(8,128)} collective-permute-done((f32[320,1024]{1,0:T(8,128)}, f32[320,1024]{1,0:T(8,128)}, u32[]{:S(2)}, u32[]{:S(2)}) %collective-permute-start.6) | collective-permute-done | bytes 1310752 | tf_op jit(solution)/shard_map/ppermute | solution.py:10
  208.3 17.3 %collective-permute-done.7 = f32[320,1024]{1,0:T(8,128)} collective-permute-done((f32[320,1024]{1,0:T(8,128)}, f32[320,1024]{1,0:T(8,128)}, u32[]{:S(2)}, u32[]{:S(2)}) %collective-permute-start.7) | collective-permute-done | bytes 1310752 | tf_op jit(solution)/shard_map/ppermute | solution.py:10
  225.7 3.5 %fusion.16 = f32[320,1024]{1,0:T(8,128)S(1)} fusion(f32[320,1024]{1,0:T(8,128)} %collective-permute-done.7, f32[320,1024]{1,0:T(8,128)} %collective-permute-done.6, f32[320,1024]{1,0:T(8,128)} %collective-permute-done.5, f32[320,1024]{1,0:T(8,128)} %collective-permute-done.4, f32[1,320,1024]{2,0,1:T(1,128)S(1)} %copy-done.4), kind=kLoop, calls=%fused_computation.23 | loop fusion | flops 1310720 | bytes 7864320 | tf_op jit(solution)/shard_map/add | solution.py:55
  229.2 1.3 add.105
  (39 shorter events, 7.5 us)
Async XLA Ops:
  7.2 126.0 %all-reduce.2.cloned.1.call-start = ((), (), s32[]{:S(2)}) async-start(), calls=%async_computation | async-start | bytes 524288 | tf_op jit(solution)/shard_map/psum | solution.py:39
  8.6 35.7 %collective-permute-start.3 = (bf16[320,1024]{1,0:T(8,128)(2,1)S(1)}, bf16[320,1024]{1,0:T(8,128)(2,1)S(1)}, u32[]{:S(2)}, u32[]{:S(2)}) collective-permute-start(bf16[320,1024]{1,0:T(8,128)(2,1)S(1)} %bitcast.79), channel_id=1, source_target_pairs={{0,112},{8,120},{16,0},{24,8},{32,16},{40,24},{48,32},{56,40},{64,... | collective-permute-start | bytes 1966088 | tf_op jit(solution)/shard_map/ppermute | solution.py:10
  14.3 29.1 %collective-permute-start.2 = (bf16[320,1024]{1,0:T(8,128)(2,1)S(1)}, bf16[320,1024]{1,0:T(8,128)(2,1)S(1)}, u32[]{:S(2)}, u32[]{:S(2)}) collective-permute-start(bf16[320,1024]{1,0:T(8,128)(2,1)S(1)} %bitcast.80), channel_id=1, source_target_pairs={{0,120},{8,0},{16,8},{24,16},{32,24},{40,32},{48,40},{56,48},{64,5... | collective-permute-start | bytes 1966088 | tf_op jit(solution)/shard_map/ppermute | solution.py:10
  15.2 26.4 %collective-permute-start.1 = (bf16[320,1024]{1,0:T(8,128)(2,1)S(1)}, bf16[320,1024]{1,0:T(8,128)(2,1)S(1)}, u32[]{:S(2)}, u32[]{:S(2)}) collective-permute-start(bf16[320,1024]{1,0:T(8,128)(2,1)S(1)} %bitcast.81), channel_id=1, source_target_pairs={{0,8},{8,16},{16,24},{24,32},{32,40},{40,48},{48,56},{56,64},{64,7... | collective-permute-start | bytes 1966088 | tf_op jit(solution)/shard_map/ppermute | solution.py:10
  16.0 24.7 %collective-permute-start = (bf16[320,1024]{1,0:T(8,128)(2,1)S(1)}, bf16[320,1024]{1,0:T(8,128)(2,1)S(1)}, u32[]{:S(2)}, u32[]{:S(2)}) collective-permute-start(bf16[320,1024]{1,0:T(8,128)(2,1)S(1)} %bitcast.82), channel_id=1, source_target_pairs={{0,16},{8,24},{16,32},{24,40},{32,48},{40,56},{48,64},{56,72},{64,... | collective-permute-start | bytes 1966088 | tf_op jit(solution)/shard_map/ppermute | solution.py:10
  48.3 6.7 %copy-start.2 = (bf16[2,10,32,1024]{3,2,1,0:T(8,128)(2,1)S(1)}, bf16[2,10,32,1024]{3,2,1,0:T(8,128)(2,1)}, u32[]{:S(2)}) copy-start(bf16[2,10,32,1024]{3,2,1,0:T(8,128)(2,1)} %param.9) | copy-start | bytes 3932164
  48.3 7.7 %copy-start.7 = (s32[1,5]{1,0:T(1,128)S(1)}, s32[1,5]{1,0:T(1,128)}, u32[]{:S(2)}) copy-start(s32[1,5]{1,0:T(1,128)} %param.11) | copy-start | bytes 64
  48.3 84.8 %copy-start.6 = (f32[32,1024]{1,0:T(8,128)S(1)}, f32[32,1024]{1,0:T(8,128)}, u32[]{:S(2)}) copy-start(f32[32,1024]{1,0:T(8,128)} %param.15) | copy-start | bytes 393220
  55.0 78.2 %copy-start.5 = (f32[2,32,1024]{2,1,0:T(8,128)S(1)}, f32[2,32,1024]{2,1,0:T(8,128)}, u32[]{:S(2)}) copy-start(f32[2,32,1024]{2,1,0:T(8,128)} %param.14) | copy-start | bytes 786436
  166.8 1.7 copy-start.1
  166.8 3.1 %copy-start = (f32[1,320,1024]{2,0,1:T(1,128)S(1)}, f32[1,320,1024]{2,0,1:T(1,128)}, u32[]{:S(2)}) copy-start(f32[1,320,1024]{2,0,1:T(1,128)} %get-tuple-element.5) | copy-start | bytes 3932164
  169.9 55.8 %copy-start.4 = (f32[1,320,1024]{2,0,1:T(1,128)S(1)}, f32[1,320,1024]{2,0,1:T(1,128)}, u32[]{:S(2)}) copy-start(f32[1,320,1024]{2,0,1:T(1,128)} %get-tuple-element.2) | copy-start | bytes 3932164
  172.6 35.6 %collective-permute-start.6 = (f32[320,1024]{1,0:T(8,128)}, f32[320,1024]{1,0:T(8,128)}, u32[]{:S(2)}, u32[]{:S(2)}) collective-permute-start(f32[320,1024]{1,0:T(8,128)} %bitcast.70), channel_id=1, source_target_pairs={{0,8},{8,16},{16,24},{24,32},{32,40},{40,48},{48,56},{56,64},{64,7... | collective-permute-start | bytes 3932168 | tf_op jit(solution)/shard_map/ppermute | solution.py:10
  179.9 45.7 %collective-permute-start.7 = (f32[320,1024]{1,0:T(8,128)}, f32[320,1024]{1,0:T(8,128)}, u32[]{:S(2)}, u32[]{:S(2)}) collective-permute-start(f32[320,1024]{1,0:T(8,128)} %bitcast.73), channel_id=1, source_target_pairs={{0,16},{8,24},{16,32},{24,40},{32,48},{40,56},{48,64},{56,72},{64,... | collective-permute-start | bytes 3932168 | tf_op jit(solution)/shard_map/ppermute | solution.py:10
  181.2 44.4 %collective-permute-start.4 = (f32[320,1024]{1,0:T(8,128)}, f32[320,1024]{1,0:T(8,128)}, u32[]{:S(2)}, u32[]{:S(2)}) collective-permute-start(f32[320,1024]{1,0:T(8,128)} %bitcast.72), channel_id=1, source_target_pairs={{0,112},{8,120},{16,0},{24,8},{32,16},{40,24},{48,32},{56,40},{64,... | collective-permute-start | bytes 3932168 | tf_op jit(solution)/shard_map/ppermute | solution.py:10
  183.5 42.2 %collective-permute-start.5 = (f32[320,1024]{1,0:T(8,128)S(1)}, f32[320,1024]{1,0:T(8,128)}, u32[]{:S(2)}, u32[]{:S(2)}) collective-permute-start(f32[320,1024]{1,0:T(8,128)S(1)} %bitcast.84), channel_id=1, source_target_pairs={{0,120},{8,0},{16,8},{24,16},{32,24},{40,32},{48,40},{56,48},{64,5... | collective-permute-start | bytes 3932168 | tf_op jit(solution)/shard_map/ppermute | solution.py:10
  225.7 3.5 %copy-start.3 = (f32[10,32,1024]{2,1,0:T(8,128)S(1)}, f32[10,32,1024]{2,1,0:T(8,128)}, u32[]{:S(2)}) copy-start(f32[10,32,1024]{2,1,0:T(8,128)} %param.8) | copy-start | bytes 3932164
Sparse Core Ops, SparseCore 0:
  56.1 76.9 all-reduce.1
where the time goes:
time: 238 us; the launch traced here: 237 us
  waiting for transfers between devices  140 us (59%)
  matrix products  32.9 us (14%)
  local copies, waits for them, and re-layouts  20.4 us (9%)
  starting transfers between devices  18.3 us (8%)
  between operations  15.5 us (7%)
  other arithmetic  10.2 us (4%)
    psum x1, waiting for transfers between devices, shards(): summed = lax.psum(partial_value, 'member')  77.1 us
    ppermute x8, waiting for transfers between devices, shifted(): return lax.ppermute(value, axis, pairs)  62.8 us
    ppermute x8, starting transfers between devices, shifted(): return lax.ppermute(value, axis, pairs)  18.3 us
    dot_general x1, matrix products, shards(): jnp.einsum('dk,krc->drc', choose, products, precision=lax.Precision.HIGHEST)  13.3 us
    dot_general x1, matrix products, shards(): jnp.einsum('rd,kcd->krc', adjoint_in, blocks[0], preferred_element_type=j...  12.9 us
    unnamed x24, local copies, waits for them, and re-layouts  9.39 us
    dot_general x1, matrix products, shards(): jnp.einsum('krc,kcd->rd', pieces, blocks[0], preferred_element_type=jnp.f...  6.62 us
    slice x1, local copies, waits for them, and re-layouts, shards(): received = by_offset[radius]  6.05 us
  transfers between devices with their start and end apart: 9, of which 4 were waited for; matrix products, arithmetic and copies ran while one was open for 3% of the time, Pallas kernels for 0%

commit v1 on v0

v1 whole, which is shorter than its diff:
```python
import functools

import jax
import jax.numpy as jnp
from jax import lax
from jax.experimental import pallas as pl
from jax.experimental.pallas import tpu as pltpu
from jax.sharding import PartitionSpec as P

MESH = pl.DeviceIdType.MESH
F32, BF16 = jnp.float32, jnp.bfloat16
CHUNKS = (8, 8, 8, 8)
COLS = 256


def kernel(tiles, groups, coeffs, perturb, blocks, neighbours, live, count, innovation, weight,
           inc_out, adj_out,
           coeff_v, pert_v, pert_f, block_v, block_t, innov_v, weight_v,
           half, zrecv, precv, loc, part, psend, mrecv, total, ain,
           csend, crecv, bsend, brecv, acc,
           load_sem, z_s, z_r, o_s, o_r, f_s, f_r, m_s, m_r, c_s, c_r, b_s, b_r):
    members, levels, width = coeffs.shape
    slots = blocks.shape[1]
    tile, group = lax.axis_index("tile"), lax.axis_index("member")
    side = 1 - 2 * lax.rem(tile, 2)

    def at(step):
        return {"tile": lax.rem(tile + step * side + tiles, tiles)}

    partner, ahead, behind = at(1), at(2), at(-2)
    peers = [{"member": lax.rem(group + d, groups)} for d in range(1, groups)]

    def remote(src, dst, send, recv, device):
        return pltpu.make_async_remote_copy(
            src_ref=src, dst_ref=dst, send_sem=send, recv_sem=recv,
            device_id=device, device_id_type=MESH)

    loads = [
        pltpu.make_async_copy(coeffs, coeff_v, load_sem.at[0]),
        pltpu.make_async_copy(perturb, pert_v, load_sem.at[1]),
        pltpu.make_async_copy(innovation, innov_v, load_sem.at[2]),
        pltpu.make_async_copy(weight, weight_v, load_sem.at[3]),
    ]
    for k in range(slots):
        loads.append(pltpu.make_async_copy(blocks.at[0, k], block_v.at[k], load_sem.at[4 + k]))
    loads[0].start()
    barrier = pltpu.get_barrier_semaphore()
    for device in [ahead, behind, partner] + peers:
        pl.semaphore_signal(barrier, inc=1, device_id=device, device_id_type=MESH)
    for load in loads[1:]:
        load.start()

    slot_at, live_at = {}, {}
    for step in range(-2, 3):
        slot, alive = jnp.int32(0), jnp.int32(0)
        for k in range(slots):
            hit = lax.rem((neighbours[0, k] - tile) * side + 2 * tiles - step, tiles) == 0
            slot = jnp.where(hit, k, slot)
            alive = jnp.where(hit, jnp.where(k < live[0], 1, 0), alive)
        slot_at[step], live_at[step] = slot, alive

    starts = [sum(CHUNKS[:c]) for c in range(len(CHUNKS))]

    def rows(c):
        return pl.ds(members * starts[c], members * CHUNKS[c])

    loads[0].wait()
    for c, size in enumerate(CHUNKS):
        lo = starts[c]
        for m in range(0, members, 2):
            two = coeff_v[m:m + 2, lo:lo + size, :].reshape(2 * size, width)
            half[pl.ds(members * lo + m * size, 2 * size)] = two.astype(BF16)

    pl.semaphore_wait(barrier, 3 + len(peers))

    pending = []

    def start(copy):
        copy.start()
        pending.append(copy)
        return copy

    zcopies, ocopies = [], []
    for c in range(len(CHUNKS)):
        r = rows(c)
        zcopies.append((
            start(remote(half.at[r], zrecv.at[0, r], z_s.at[0, c], z_r.at[0, c], behind)),
            start(remote(half.at[r], zrecv.at[1, r], z_s.at[1, c], z_r.at[1, c], ahead))))
        ocopies.append(start(remote(half.at[r], precv.at[0, r], o_s.at[c], o_r.at[c], partner)))

    def forward(piece, r, step, first=False):
        value = piece[...]
        for n in range(0, width, COLS):
            product = jnp.dot(value, block_v[slot_at[step], :, n:n + COLS], preferred_element_type=F32)
            product = jnp.where(live_at[step] > 0, product, 0.0)
            loc[r, n:n + COLS] = product if first else loc[r, n:n + COLS] + product

    loads[1].wait()
    for t in range(2):
        for m in range(members):
            pert_f[t, m] = pert_v[t, m].astype(F32)
    for load in loads[4:]:
        load.wait()
    everything = pl.ds(0, members * levels)
    forward(half, everything, 0, first=True)
    for k in range(slots):
        for n in range(0, width, COLS):
            block_t[k, :, n:n + COLS] = block_v[k, n:n + COLS, :].T
    for copy in ocopies:
        copy.wait_recv()
    forward(precv.at[0], everything, 1)
    loads[2].wait()
    loads[3].wait()

    mcopies = {}

    def contract(c):
        r, lo, size = rows(c), starts[c], CHUNKS[c]
        near, far = zcopies[c]
        near.wait_recv()
        passed = start(remote(zrecv.at[0, r], precv.at[1, r], f_s.at[c], f_r.at[c], partner))
        forward(zrecv.at[0, r], r, 2)
        far.wait_recv()
        forward(zrecv.at[1, r], r, -2)
        passed.wait_recv()
        forward(precv.at[1, r], r, -1)
        for t in range(2):
            value = jnp.zeros((size, width), F32)
            for m in range(members):
                value = value + pert_f[t, m, lo:lo + size, :] * loc[pl.ds(members * lo + m * size, size)]
            part[t, lo:lo + size, :] = value
        both = part[:, lo:lo + size, :].reshape(2 * size, width)
        mine = pl.ds(2 * lo, 2 * size)
        psend[mine] = both.astype(BF16)
        mcopies[c] = [
            start(remote(psend.at[mine], mrecv.at[d, mine], m_s.at[d, c], m_r.at[d, c], peers[d]))
            for d in range(len(peers))]

    column = lax.broadcasted_iota(jnp.int32, (1, 1, width), 2)
    observed = column < count[0]
    bcopies, kept = {}, {}

    def product(value, step, n):
        out = jnp.dot(value, block_t[slot_at[step], :, n:n + COLS], preferred_element_type=F32)
        return jnp.where(live_at[step] > 0, out, 0.0)

    def adjoint(c):
        r, lo, size = rows(c), starts[c], CHUNKS[c]
        mine = pl.ds(2 * lo, 2 * size)
        for copy in mcopies[c]:
            copy.wait_recv()
        summed = part[:, lo:lo + size, :]
        for d in range(len(peers)):
            summed = summed + mrecv[d, mine].astype(F32).reshape(2, size, width)
        total[:, lo:lo + size, :] = summed
        residual = weight_v[lo:lo + size, :][None] * jnp.where(
            observed, summed - innov_v[:, lo:lo + size, :], 0.0)
        for m in range(0, members, 2):
            two = pert_f[0, m:m + 2, lo:lo + size, :] * residual[0][None]
            two = two + pert_f[1, m:m + 2, lo:lo + size, :] * residual[1][None]
            ain[pl.ds(members * lo + m * size, 2 * size)] = two.reshape(2 * size, width).astype(BF16)
        value = ain[r]
        for n in range(0, width, COLS):
            csend[0, r, n:n + COLS] = product(value, -1, n).astype(BF16)
        shared = start(remote(csend.at[0, r], crecv.at[0, r], c_s.at[0, c], c_r.at[0, c], partner))
        for n in range(0, width, COLS):
            bsend[0, r, n:n + COLS] = product(value, -2, n).astype(BF16)
        lone = start(remote(bsend.at[0, r], brecv.at[0, r], b_s.at[0, c], b_r.at[0, c], behind))
        for n in range(0, width, COLS):
            acc[r, n:n + COLS] = product(value, 2, n)
        shared.wait_recv()
        bsend[1, r] = (acc[r] + crecv[0, r].astype(F32)).astype(BF16)
        pair = start(remote(bsend.at[1, r], brecv.at[1, r], b_s.at[1, c], b_r.at[1, c], ahead))
        for n in range(0, width, COLS):
            csend[1, r, n:n + COLS] = product(value, 1, n).astype(BF16)
        given = start(remote(csend.at[1, r], crecv.at[1, r], c_s.at[1, c], c_r.at[1, c], partner))
        for n in range(0, width, COLS):
            acc[r, n:n + COLS] = product(value, 0, n)
        bcopies[c] = (given, lone, pair)

    def finish(c):
        lo, size = starts[c], CHUNKS[c]
        for copy in bcopies[c]:
            copy.wait_recv()
        for m in range(0, members, 2):
            r = pl.ds(members * lo + m * size, 2 * size)
            value = acc[r] + crecv[1, r].astype(F32)
            value = value + (brecv[0, r].astype(F32) + brecv[1, r].astype(F32))
            adj_out[m:m + 2, lo:lo + size, :] = value.reshape(2, size, width)

    order = [("c", 0), ("c", 1), ("c", 2), ("a", 0), ("c", 3), ("a", 1), ("a", 2), ("a", 3)]
    for kind, c in order:
        (contract if kind == "c" else adjoint)(c)
    own = pl.multiple_of(group * (width // groups), width // groups)
    inc_out[...] = total[:, :, pl.ds(own, width // groups)]
    for c in range(len(CHUNKS)):
        finish(c)
    for copy in pending:
        copy.wait_send()


def shards(coeffs, perturb, blocks, neighbours, live, obs_count, innovation, obs_weight):
    members, levels, width = coeffs.shape
    slots = blocks.shape[1]
    tiles, groups = lax.axis_size("tile"), lax.axis_size("member")
    row_count, chunks, peers = members * levels, len(CHUNKS), groups - 1
    anywhere = pl.BlockSpec(memory_space=pl.ANY)
    scalars = pl.BlockSpec(memory_space=pltpu.SMEM)
    vmem = pl.BlockSpec(memory_space=pltpu.VMEM)
    dma = pltpu.SemaphoreType.DMA
    increment, adjoint = pl.pallas_call(
        functools.partial(kernel, tiles, groups),
        out_shape=(
            jax.ShapeDtypeStruct((2, levels, width // groups), F32),
            jax.ShapeDtypeStruct((members, levels, width), F32),
        ),
        in_specs=[anywhere, anywhere, anywhere, scalars, scalars, scalars, anywhere, anywhere],
        out_specs=(vmem, vmem),
        scratch_shapes=[
            pltpu.VMEM((members, levels, width), F32),
            pltpu.VMEM((2, members, levels, width), BF16),
            pltpu.VMEM((2, members, levels, width), F32),
            pltpu.VMEM((slots, width, width), BF16),
            pltpu.VMEM((slots, width, width), BF16),
            pltpu.VMEM((2, levels, width), F32),
            pltpu.VMEM((levels, width), F32),
            pltpu.VMEM((row_count, width), BF16),
            pltpu.VMEM((2, row_count, width), BF16),
            pltpu.VMEM((2, row_count, width), BF16),
            pltpu.VMEM((row_count, width), F32),
            pltpu.VMEM((2, levels, width), F32),
            pltpu.VMEM((2 * levels, width), BF16),
            pltpu.VMEM((peers, 2 * levels, width), BF16),
            pltpu.VMEM((2, levels, width), F32),
            pltpu.VMEM((row_count, width), BF16),
            pltpu.VMEM((2, row_count, width), BF16),
            pltpu.VMEM((2, row_count, width), BF16),
            pltpu.VMEM((2, row_count, width), BF16),
            pltpu.VMEM((2, row_count, width), BF16),
            pltpu.VMEM((row_count, width), F32),
            dma((4 + slots,)),
            dma((2, chunks)), dma((2, chunks)),
            dma((chunks,)), dma((chunks,)),
            dma((chunks,)), dma((chunks,)),
            dma((peers, chunks)), dma((peers, chunks)),
            dma((2, chunks)), dma((2, chunks)),
            dma((2, chunks)), dma((2, chunks)),
        ],
        compiler_params=pltpu.CompilerParams(
            collective_id=0, has_side_effects=True, vmem_limit_bytes=56 * 1024 * 1024),
        cost_estimate=pl.CostEstimate(
            flops=4 * row_count * width * width * slots, bytes_accessed=16 * 1024 * 1024, transcendentals=0),
    )(coeffs, perturb, blocks, neighbours, live, obs_count, innovation, obs_weight)
    return increment, coeffs + adjoint


def solution(mesh):
    placed = (
        P("member", None, "tile"),
        P(None, "member", None, "tile"),
        P("tile", None, None, None),
        P("tile", None),
        P("tile"),
        P("tile"),
        P(None, None, "tile"),
        P(None, "tile"),
    )
    return jax.shard_map(
        shards,
        mesh=mesh,
        in_specs=placed,
        out_specs=(P(None, None, ("tile", "member")), P("member", None, "tile")),
        check_vma=False,
    )
```

time: 238 us -> 60.2 us (0.25)
  the two profiles are of different devices: /device:TPU:1 before, /device:TPU:16 now
where the time goes in v1:
time: 60.2 us; the launch traced here: 60.1 us
  Pallas kernels  54.9 us (91%)
  other arithmetic  2.64 us (4%)
  between operations  1.96 us (3%)
  local copies, waits for them, and re-layouts  0.62 us (1%)
    pallas_call x1, Pallas kernels, shards(): pl.pallas_call(functools.partial(kernel, tiles, groups), out_shape=(jax.S...  54.9 us
    add x1, other arithmetic, shards(): return (increment, coeffs + adjoint)  2.64 us

profile of v1, /device:TPU:16, one launch (start us, length us, event | category | flops | bytes accessed | tf_op | source)
XLA Modules:
  0.0 60.1 jit_solution(14230407270014831643)
XLA Ops:
  1.9 0.0 copy-start
  1.9 54.9 %shard_map.95 = (f32[2,32,128]{2,1,0:T(8,128)}, f32[10,32,1024]{2,1,0:T(8,128)}) custom-call(f32[10,32,1024]{2,1,0:T(8,128)} %coeffs.1, bf16[2,10,32,1024]{3,2,1,0:T(8,128)(2,1)} %perturb.1, bf16[1,5,1024,1024]{3,2,1,0:T(8,128)(2,1)} %blocks.1, s32[1,5]{1,0:T(1,128)} %neighbours.1, s32[1]{0:T(128)S(6)} %copy.11.live, s32[1]{0:T(128)S(6)} %copy.12.count, ...), custom_call_target="tpu_custom_call" | custom-call | flops 6710886400 | bytes 16777216 | tf_op jit(solution)/shard_map/pallas_call | solution.py:211
  56.8 0.0 copy-done
  56.8 0.0 copy-start.1
  56.8 2.6 %add.3 = f32[10,32,1024]{2,1,0:T(8,128)} add(f32[10,32,1024]{2,1,0:T(8,128)S(1)} %copy-done, f32[10,32,1024]{2,1,0:T(8,128)} %get-tuple-element.5) | non-fusion elementwise | flops 327680 | bytes 3932160 | tf_op jit(solution)/shard_map/add | solution.py:254
  59.5 0.0 copy-done.1
  59.5 0.6 %copy.13 = f32[2,32,128]{2,1,0:T(8,128)} copy(f32[2,32,128]{2,1,0:T(8,128)S(1)} %copy-done.1) | data formatting | bytes 65536
Async XLA Ops:
  1.9 54.9 %copy-start = (f32[10,32,1024]{2,1,0:T(8,128)S(1)}, f32[10,32,1024]{2,1,0:T(8,128)}, u32[]{:S(2)}) copy-start(f32[10,32,1024]{2,1,0:T(8,128)} %coeffs.1) | copy-start | bytes 3932164
  56.8 2.6 %copy-start.1 = (f32[2,32,128]{2,1,0:T(8,128)S(1)}, f32[2,32,128]{2,1,0:T(8,128)}, u32[]{:S(2)}) copy-start(f32[2,32,128]{2,1,0:T(8,128)} %get-tuple-element.8) | copy-start | bytes 98308

commit v2 on v1

--- a/solution.py
+++ b/solution.py
@@ -10,15 +10,21 @@
 MESH = pl.DeviceIdType.MESH
 F32, BF16 = jnp.float32, jnp.bfloat16
 CHUNKS = (8, 8, 8, 8)
+X_FIRST = (0, 1)
+ORDER = (
+    "z0", "t0", "x0", "z1", "t1", "x1", "z2", "t2", "m0", "x2", "z3", "t3",
+    "m1", "x3", "t4", "m2", "a0", "m3", "a1", "a2", "a3",
+)
 COLS = 256
 
 
-def kernel(tiles, groups, coeffs, perturb, blocks, neighbours, live, count, innovation, weight,
-           inc_out, adj_out,
+def kernel(tiles, groups, coeffs, perturb, blocks, neighbours_in, live_in, count_in, innovation, weight,
+           inc_out, grad_out,
            coeff_v, pert_v, pert_f, block_v, block_t, innov_v, weight_v,
-           half, zrecv, precv, loc, part, psend, mrecv, total, ain,
+           half, zrecv, precv, loc, part, psend, xrecv, ysend, yrecv, total, ain,
            csend, crecv, bsend, brecv, acc,
-           load_sem, z_s, z_r, o_s, o_r, f_s, f_r, m_s, m_r, c_s, c_r, b_s, b_r):
+           neighbours, live, count, scalar_sem,
+           load_sem, z_s, z_r, o_s, o_r, f_s, f_r, m_s, m_r, g_s, g_r, c_s, c_r, b_s, b_r):
     members, levels, width = coeffs.shape
     slots = blocks.shape[1]
     tile, group = lax.axis_index("tile"), lax.axis_index("member")
@@ -28,28 +34,71 @@
         return {"tile": lax.rem(tile + step * side + tiles, tiles)}
 
     partner, ahead, behind = at(1), at(2), at(-2)
-    peers = [{"member": lax.rem(group + d, groups)} for d in range(1, groups)]
+    line = groups // 2
+    place = lax.rem(group, line)
+    peers = [{"member": group - place + lax.rem(place + d, line)} for d in range(1, line)]
+    across = {"member": lax.rem(group + line, groups)}
 
     def remote(src, dst, send, recv, device):
         return pltpu.make_async_remote_copy(
             src_ref=src, dst_ref=dst, send_sem=send, recv_sem=recv,
             device_id=device, device_id_type=MESH)
 
+    first = [pltpu.make_async_copy(coeffs.at[m], coeff_v.at[m], load_sem.at[4 + slots + m]) for m in range(members)]
+    scalars = [
+        pltpu.make_async_copy(neighbours_in, neighbours, scalar_sem.at[0]),
+        pltpu.make_async_copy(live_in, live, scalar_sem.at[1]),
+        pltpu.make_async_copy(count_in, count, scalar_sem.at[2]),
+    ]
     loads = [
-        pltpu.make_async_copy(coeffs, coeff_v, load_sem.at[0]),
-        pltpu.make_async_copy(perturb, pert_v, load_sem.at[1]),
+        pltpu.make_async_copy(perturb.at[0], pert_v.at[0], load_sem.at[0]),
+        pltpu.make_async_copy(perturb.at[1], pert_v.at[1], load_sem.at[1]),
         pltpu.make_async_copy(innovation, innov_v, load_sem.at[2]),
         pltpu.make_async_copy(weight, weight_v, load_sem.at[3]),
     ]
     for k in range(slots):
         loads.append(pltpu.make_async_copy(blocks.at[0, k], block_v.at[k], load_sem.at[4 + k]))
-    loads[0].start()
     barrier = pltpu.get_barrier_semaphore()
-    for device in [ahead, behind, partner] + peers:
+    for device in [ahead, behind, partner, across] + peers:
         pl.semaphore_signal(barrier, inc=1, device_id=device, device_id_type=MESH)
-    for load in loads[1:]:
+    for load in first + scalars:
         load.start()
 
+    starts = [sum(CHUNKS[:c]) for c in range(len(CHUNKS))]
+
+    def rows(c):
+        return pl.ds(members * starts[c], members * CHUNKS[c])
+
+    for load in first:
+        load.wait()
+    for c, size in enumerate(CHUNKS):
+        lo = starts[c]
+        for m in range(0, members, 2):
+            two = coeff_v[m:m + 2, lo:lo + size, :].reshape(2 * size, width)
+            half[pl.ds(members * lo + m * size, 2 * size)] = two.astype(BF16)
+
+    pl.semaphore_wait(barrier, 4 + len(peers))
+
+    pending = []
+
+    def start(copy):
+        copy.start()
+        pending.append(copy)
+        return copy
+
+    zcopies, ocopies = [], []
+    for c in range(len(CHUNKS)):
+        r = rows(c)
+        zcopies.append((
+            start(remote(half.at[r], zrecv.at[0, r], z_s.at[0, c], z_r.at[0, c], behind)),
+            start(remote(half.at[r], zrecv.at[1, r], z_s.at[1, c], z_r.at[1, c], ahead))))
+        if c == 0:
+            for load in loads:
+                load.start()
+        ocopies.append(start(remote(half.at[r], precv.at[0, r], o_s.at[c], o_r.at[c], partner)))
+
+    for load in scalars:
+        load.wait()
     slot_at, live_at = {}, {}
     for step in range(-2, 3):
         slot, alive = jnp.int32(0), jnp.int32(0)
@@ -59,35 +108,6 @@
             alive = jnp.where(hit, jnp.where(k < live[0], 1, 0), alive)
         slot_at[step], live_at[step] = slot, alive
 
-    starts = [sum(CHUNKS[:c]) for c in range(len(CHUNKS))]
-
-    def rows(c):
-        return pl.ds(members * starts[c], members * CHUNKS[c])
-
-    loads[0].wait()
-    for c, size in enumerate(CHUNKS):
-        lo = starts[c]
-        for m in range(0, members, 2):
-            two = coeff_v[m:m + 2, lo:lo + size, :].reshape(2 * size, width)
-            half[pl.ds(members * lo + m * size, 2 * size)] = two.astype(BF16)
-
-    pl.semaphore_wait(barrier, 3 + len(peers))
-
-    pending = []
-
-    def start(copy):
-        copy.start()
-        pending.append(copy)
-        return copy
-
-    zcopies, ocopies = [], []
-    for c in range(len(CHUNKS)):
-        r = rows(c)
-        zcopies.append((
-            start(remote(half.at[r], zrecv.at[0, r], z_s.at[0, c], z_r.at[0, c], behind)),
-            start(remote(half.at[r], zrecv.at[1, r], z_s.at[1, c], z_r.at[1, c], ahead))))
-        ocopies.append(start(remote(half.at[r], precv.at[0, r], o_s.at[c], o_r.at[c], partner)))
-
     def forward(piece, r, step, first=False):
         value = piece[...]
         for n in range(0, width, COLS):
@@ -95,6 +115,7 @@
             product = jnp.where(live_at[step] > 0, product, 0.0)
             loc[r, n:n + COLS] = product if first else loc[r, n:n + COLS] + product
 
+    loads[0].wait()
     loads[1].wait()
     for t in range(2):
         for m in range(members):
@@ -103,26 +124,31 @@
         load.wait()
     everything = pl.ds(0, members * levels)
     forward(half, everything, 0, first=True)
-    for k in range(slots):
+
+    def turn(k):
         for n in range(0, width, COLS):
             block_t[k, :, n:n + COLS] = block_v[k, n:n + COLS, :].T
+
     for copy in ocopies:
         copy.wait_recv()
     forward(precv.at[0], everything, 1)
     loads[2].wait()
     loads[3].wait()
 
-    mcopies = {}
-
-    def contract(c):
-        r, lo, size = rows(c), starts[c], CHUNKS[c]
+    xcopies, ycopies, passing = {}, {}, {}
+
+    def arrive(c):
+        r = rows(c)
         near, far = zcopies[c]
         near.wait_recv()
-        passed = start(remote(zrecv.at[0, r], precv.at[1, r], f_s.at[c], f_r.at[c], partner))
+        passing[c] = start(remote(zrecv.at[0, r], precv.at[1, r], f_s.at[c], f_r.at[c], partner))
         forward(zrecv.at[0, r], r, 2)
         far.wait_recv()
         forward(zrecv.at[1, r], r, -2)
-        passed.wait_recv()
+
+    def contract(c):
+        r, lo, size = rows(c), starts[c], CHUNKS[c]
+        passing[c].wait_recv()
         forward(precv.at[1, r], r, -1)
         for t in range(2):
             value = jnp.zeros((size, width), F32)
@@ -132,9 +158,38 @@
         both = part[:, lo:lo + size, :].reshape(2 * size, width)
         mine = pl.ds(2 * lo, 2 * size)
         psend[mine] = both.astype(BF16)
-        mcopies[c] = [
-            start(remote(psend.at[mine], mrecv.at[d, mine], m_s.at[d, c], m_r.at[d, c], peers[d]))
+        (along if c in X_FIRST else beyond)(c, psend)
+
+    def along(c, source):
+        mine = pl.ds(2 * starts[c], 2 * CHUNKS[c])
+        xcopies[c] = [
+            start(remote(source.at[mine], xrecv.at[d, mine], m_s.at[d, c], m_r.at[d, c], peers[d]))
             for d in range(len(peers))]
+
+    def beyond(c, source):
+        mine = pl.ds(2 * starts[c], 2 * CHUNKS[c])
+        ycopies[c] = start(remote(source.at[mine], yrecv.at[mine], g_s.at[c], g_r.at[c], across))
+
+    def with_line(c, summed):
+        mine = pl.ds(2 * starts[c], 2 * CHUNKS[c])
+        for copy in xcopies[c]:
+            copy.wait_recv()
+        for d in range(len(peers)):
+            summed = summed + xrecv[d, mine].astype(F32)
+        return summed
+
+    def with_across(c, summed):
+        ycopies[c].wait_recv()
+        return summed + yrecv[pl.ds(2 * starts[c], 2 * CHUNKS[c])].astype(F32)
+
+    def merge(c):
+        lo, size = starts[c], CHUNKS[c]
+        mine = pl.ds(2 * lo, 2 * size)
+        summed = part[:, lo:lo + size, :].reshape(2 * size, width)
+        summed = (with_line if c in X_FIRST else with_across)(c, summed)
+        part[:, lo:lo + size, :] = summed.reshape(2, size, width)
+        ysend[mine] = summed.astype(BF16)
+        (beyond if c in X_FIRST else along)(c, ysend)
 
     column = lax.broadcasted_iota(jnp.int32, (1, 1, width), 2)
     observed = column < count[0]
@@ -146,12 +201,8 @@
 
     def adjoint(c):
         r, lo, size = rows(c), starts[c], CHUNKS[c]
-        mine = pl.ds(2 * lo, 2 * size)
-        for copy in mcopies[c]:
-            copy.wait_recv()
-        summed = part[:, lo:lo + size, :]
-        for d in range(len(peers)):
-            summed = summed + mrecv[d, mine].astype(F32).reshape(2, size, width)
+        summed = part[:, lo:lo + size, :].reshape(2 * size, width)
+        summed = (with_across if c in X_FIRST else with_line)(c, summed).reshape(2, size, width)
         total[:, lo:lo + size, :] = summed
         residual = weight_v[lo:lo + size, :][None] * jnp.where(
             observed, summed - innov_v[:, lo:lo + size, :], 0.0)
@@ -185,12 +236,13 @@
         for m in range(0, members, 2):
             r = pl.ds(members * lo + m * size, 2 * size)
             value = acc[r] + crecv[1, r].astype(F32)
+            value = value + coeff_v[m:m + 2, lo:lo + size, :].reshape(2 * size, width)
             value = value + (brecv[0, r].astype(F32) + brecv[1, r].astype(F32))
-            adj_out[m:m + 2, lo:lo + size, :] = value.reshape(2, size, width)
-
-    order = [("c", 0), ("c", 1), ("c", 2), ("a", 0), ("c", 3), ("a", 1), ("a", 2), ("a", 3)]
-    for kind, c in order:
-        (contract if kind == "c" else adjoint)(c)
+            grad_out[m:m + 2, lo:lo + size, :] = value.reshape(2, size, width)
+
+    steps = {"z": arrive, "x": contract, "m": merge, "a": adjoint, "t": turn}
+    for step in ORDER:
+        steps[step[0]](int(step[1:]))
     own = pl.multiple_of(group * (width // groups), width // groups)
     inc_out[...] = total[:, :, pl.ds(own, width // groups)]
     for c in range(len(CHUNKS)):
@@ -203,18 +255,17 @@
     members, levels, width = coeffs.shape
     slots = blocks.shape[1]
     tiles, groups = lax.axis_size("tile"), lax.axis_size("member")
-    row_count, chunks, peers = members * levels, len(CHUNKS), groups - 1
+    row_count, chunks, peers = members * levels, len(CHUNKS), groups // 2 - 1
     anywhere = pl.BlockSpec(memory_space=pl.ANY)
-    scalars = pl.BlockSpec(memory_space=pltpu.SMEM)
     vmem = pl.BlockSpec(memory_space=pltpu.VMEM)
     dma = pltpu.SemaphoreType.DMA
-    increment, adjoint = pl.pallas_call(
+    held = pl.pallas_call(
         functools.partial(kernel, tiles, groups),
         out_shape=(
-            jax.ShapeDtypeStruct((2, levels, width // groups), F32),
-            jax.ShapeDtypeStruct((members, levels, width), F32),
+            pltpu.VMEM((2, levels, width // groups), F32),
+            pltpu.VMEM((members, levels, width), F32),
         ),
-        in_specs=[anywhere, anywhere, anywhere, scalars, scalars, scalars, anywhere, anywhere],
+        in_specs=[anywhere] * 8,
         out_specs=(vmem, vmem),
         scratch_shapes=[
             pltpu.VMEM((members, levels, width), F32),
@@ -231,6 +282,8 @@
             pltpu.VMEM((2, levels, width), F32),
             pltpu.VMEM((2 * levels, width), BF16),
             pltpu.VMEM((peers, 2 * levels, width), BF16),
+            pltpu.VMEM((2 * levels, width), BF16),
+            pltpu.VMEM((2 * levels, width), BF16),
             pltpu.VMEM((2, levels, width), F32),
             pltpu.VMEM((row_count, width), BF16),
             pltpu.VMEM((2, row_count, width), BF16),
@@ -238,11 +291,16 @@
             pltpu.VMEM((2, row_count, width), BF16),
             pltpu.VMEM((2, row_count, width), BF16),
             pltpu.VMEM((row_count, width), F32),
-            dma((4 + slots,)),
+            pltpu.SMEM((1, slots), jnp.int32),
+            pltpu.SMEM((1,), jnp.int32),
+            pltpu.SMEM((1,), jnp.int32),
+            dma((3,)),
+            dma((members + 4 + slots,)),
             dma((2, chunks)), dma((2, chunks)),
             dma((chunks,)), dma((chunks,)),
             dma((chunks,)), dma((chunks,)),
             dma((peers, chunks)), dma((peers, chunks)),
+            dma((chunks,)), dma((chunks,)),
             dma((2, chunks)), dma((2, chunks)),
             dma((2, chunks)), dma((2, chunks)),
         ],
@@ -251,7 +309,7 @@
         cost_estimate=pl.CostEstimate(
             flops=4 * row_count * width * width * slots, bytes_accessed=16 * 1024 * 1024, transcendentals=0),
     )(coeffs, perturb, blocks, neighbours, live, obs_count, innovation, obs_weight)
-    return increment, coeffs + adjoint
+    return held
 
 
 def solution(mesh):

time: 60.2 us -> 48.7 us (0.81)
  the two profiles are of different devices: /device:TPU:16 before, /device:TPU:1 now
where the time goes in v2:
time: 48.7 us; the launch traced here: 48.6 us
  Pallas kernels  45 us (92%)
  between operations  1.93 us (4%)
  local copies, waits for them, and re-layouts  1.67 us (3%)
    pallas_call x1, Pallas kernels, shards(): pl.pallas_call(functools.partial(kernel, tiles, groups), out_shape=(pltpu...  45 us
    unnamed x2, local copies, waits for them, and re-layouts  1.67 us

profile of v2, /device:TPU:1, one launch (start us, length us, event | category | flops | bytes accessed | tf_op | source)
XLA Modules:
  0.0 48.6 jit_solution(8319506305441455397)
XLA Ops:
  1.9 45.0 %shard_map.95 = (f32[2,32,128]{2,1,0:T(8,128)S(1)}, f32[10,32,1024]{2,1,0:T(8,128)S(1)}) custom-call(f32[10,32,1024]{2,1,0:T(8,128)} %coeffs.1, bf16[2,10,32,1024]{3,2,1,0:T(8,128)(2,1)} %perturb.1, bf16[1,5,1024,1024]{3,2,1,0:T(8,128)(2,1)} %blocks.1, s32[1,5]{1,0:T(1,128)} %neighbours_in.1, s32[1]{0:T(128)S(6)} %copy.14.live_in, s32[1]{0:T(128)S(6)} %copy.15.count_in, ...), custom_call_target="tpu_custom_call" | custom-call | flops 6710886400 | bytes 16777216 | tf_op jit(solution)/shard_map/pallas_call | solution.py:262
  46.9 0.6 %copy.12 = f32[2,32,128]{2,1,0:T(8,128)} copy(f32[2,32,128]{2,1,0:T(8,128)S(1)} %get-tuple-element.2) | data formatting | bytes 65536
  47.5 1.1 %copy.13 = f32[10,32,1024]{2,1,0:T(8,128)} copy(f32[10,32,1024]{2,1,0:T(8,128)S(1)} %get-tuple-element.3) | data formatting | bytes 2621440

commit v3 on v2

--- a/solution.py
+++ b/solution.py
@@ -12,8 +12,8 @@
 CHUNKS = (8, 8, 8, 8)
 X_FIRST = (0, 1)
 ORDER = (
-    "z0", "t0", "x0", "z1", "t1", "x1", "z2", "t2", "m0", "x2", "z3", "t3",
-    "m1", "x3", "t4", "m2", "a0", "m3", "a1", "a2", "a3",
+    "z0", "t0", "x0", "t1", "z1", "t2", "x1", "t3", "z2", "m0", "x2", "t4", "z3", "x3",
+    "m1", "a0", "m2", "b0", "m3", "a1", "b1", "a2", "b2", "a3", "b3",
 )
 COLS = 256
 
@@ -193,7 +193,7 @@
 
     column = lax.broadcasted_iota(jnp.int32, (1, 1, width), 2)
     observed = column < count[0]
-    bcopies, kept = {}, {}
+    shares, lones, pairs = {}, {}, {}
 
     def product(value, step, n):
         out = jnp.dot(value, block_t[slot_at[step], :, n:n + COLS], preferred_element_type=F32)
@@ -219,20 +219,33 @@
         lone = start(remote(bsend.at[0, r], brecv.at[0, r], b_s.at[0, c], b_r.at[0, c], behind))
         for n in range(0, width, COLS):
             acc[r, n:n + COLS] = product(value, 2, n)
-        shared.wait_recv()
+        shares[c], lones[c] = shared, lone
+
+    def pair(c):
+        r = rows(c)
+        shares[c].wait_recv()
         bsend[1, r] = (acc[r] + crecv[0, r].astype(F32)).astype(BF16)
-        pair = start(remote(bsend.at[1, r], brecv.at[1, r], b_s.at[1, c], b_r.at[1, c], ahead))
-        for n in range(0, width, COLS):
-            csend[1, r, n:n + COLS] = product(value, 1, n).astype(BF16)
-        given = start(remote(csend.at[1, r], crecv.at[1, r], c_s.at[1, c], c_r.at[1, c], partner))
-        for n in range(0, width, COLS):
-            acc[r, n:n + COLS] = product(value, 0, n)
-        bcopies[c] = (given, lone, pair)
+        pairs[c] = start(remote(bsend.at[1, r], brecv.at[1, r], b_s.at[1, c], b_r.at[1, c], ahead))
+
+    def rest():
+        given = []
+        count_half = members * levels // 2
+        for part_id in range(2):
+            r = pl.ds(part_id * count_half, count_half)
+            value = ain[r]
+            for n in range(0, width, COLS):
+                csend[1, r, n:n + COLS] = product(value, 1, n).astype(BF16)
+            given.append(start(remote(csend.at[1, r], crecv.at[1, r], c_s.at[1, part_id], c_r.at[1, part_id], partner)))
+        value = ain[...]
+        for n in range(0, width, COLS):
+            acc[:, n:n + COLS] = product(value, 0, n)
+        for copy in given:
+            copy.wait_recv()
 
     def finish(c):
         lo, size = starts[c], CHUNKS[c]
-        for copy in bcopies[c]:
-            copy.wait_recv()
+        lones[c].wait_recv()
+        pairs[c].wait_recv()
         for m in range(0, members, 2):
             r = pl.ds(members * lo + m * size, 2 * size)
             value = acc[r] + crecv[1, r].astype(F32)
@@ -240,15 +253,26 @@
             value = value + (brecv[0, r].astype(F32) + brecv[1, r].astype(F32))
             grad_out[m:m + 2, lo:lo + size, :] = value.reshape(2, size, width)
 
-    steps = {"z": arrive, "x": contract, "m": merge, "a": adjoint, "t": turn}
+    steps = {"z": arrive, "x": contract, "m": merge, "a": adjoint, "b": pair, "t": turn}
     for step in ORDER:
         steps[step[0]](int(step[1:]))
     own = pl.multiple_of(group * (width // groups), width // groups)
     inc_out[...] = total[:, :, pl.ds(own, width // groups)]
+    rest()
     for c in range(len(CHUNKS)):
         finish(c)
     for copy in pending:
         copy.wait_send()
+
+
+def write(inc, grad, inc_out, grad_out, sem):
+    members = grad.shape[0]
+    copies = [pltpu.make_async_copy(inc, inc_out, sem.at[members])]
+    copies += [pltpu.make_async_copy(grad.at[m], grad_out.at[m], sem.at[m]) for m in range(members)]
+    for copy in copies:
+        copy.start()
+    for copy in copies:
+        copy.wait()
 
 
 def shards(coeffs, perturb, blocks, neighbours, live, obs_count, innovation, obs_weight):
@@ -309,7 +333,14 @@
         cost_estimate=pl.CostEstimate(
             flops=4 * row_count * width * width * slots, bytes_accessed=16 * 1024 * 1024, transcendentals=0),
     )(coeffs, perturb, blocks, neighbours, live, obs_count, innovation, obs_weight)
-    return held
+    held = [pltpu.with_memory_space_constraint(x, pltpu.VMEM) for x in held]
+    return pl.pallas_call(
+        write,
+        out_shape=tuple(jax.ShapeDtypeStruct(x.shape, x.dtype) for x in held),
+        in_specs=[anywhere, anywhere],
+        out_specs=(anywhere, anywhere),
+        scratch_shapes=[dma((members + 1,))],
+    )(*held)
 
 
 def solution(mesh):

time: 48.7 us -> 47.4 us (0.973)
  local copies, waits for them, and re-layouts: 1.67 us -> 0 us
    unnamed x2 -> x0, local copies, waits for them, and re-layouts: 1.67 us -> none
    pallas_call x0 -> x1, Pallas kernels: none -> 1.15 us  [shards(): pl.pallas_call(write, out_shape=tuple((jax.ShapeDtypeStruct(x.shape, x.dt...]
    pallas_call x1, Pallas kernels: 45 us -> 44.2 us  [shards(): pl.pallas_call(functools.partial(kernel, tiles, groups), out_shape=(pltpu...]
where the time goes in v3:
time: 47.4 us; the launch traced here: 47.3 us
  Pallas kernels  45.4 us (96%)
  between operations  1.93 us (4%)
    pallas_call x1, Pallas kernels, shards(): pl.pallas_call(functools.partial(kernel, tiles, groups), out_shape=(pltpu...  44.2 us
    pallas_call x1, Pallas kernels, shards(): pl.pallas_call(write, out_shape=tuple((jax.ShapeDtypeStruct(x.shape, x.dt...  1.15 us

profile of v3, /device:TPU:1, one launch (start us, length us, event | category | flops | bytes accessed | tf_op | source)
XLA Modules:
  0.0 47.3 jit_solution(16537709278647059413)
XLA Ops:
  1.9 44.2 %shard_map.95 = (f32[2,32,128]{2,1,0:T(8,128)S(1)}, f32[10,32,1024]{2,1,0:T(8,128)S(1)}) custom-call(f32[10,32,1024]{2,1,0:T(8,128)} %coeffs.1, bf16[2,10,32,1024]{3,2,1,0:T(8,128)(2,1)} %perturb.1, bf16[1,5,1024,1024]{3,2,1,0:T(8,128)(2,1)} %blocks.1, s32[1,5]{1,0:T(1,128)} %neighbours_in.1, s32[1]{0:T(128)S(6)} %copy.10.live_in, s32[1]{0:T(128)S(6)} %copy.11.count_in, ...), custom_call_target="tpu_custom_call" | custom-call | flops 6710886400 | bytes 16777216 | tf_op jit(solution)/shard_map/pallas_call | solution.py:286
  46.1 1.1 %shard_map.96 = (f32[2,32,128]{2,1,0:T(8,128)}, f32[10,32,1024]{2,1,0:T(8,128)}) custom-call(f32[2,32,128]{2,1,0:T(8,128)S(1)} %get-tuple-element.4.inc, f32[10,32,1024]{2,1,0:T(8,128)S(1)} %get-tuple-element.5.grad), custom_call_target="tpu_custom_call" | custom-call | tf_op jit(solution)/shard_map/pallas_call | solution.py:337

commit v4 on v3

--- a/solution.py
+++ b/solution.py
@@ -12,8 +12,8 @@
 CHUNKS = (8, 8, 8, 8)
 X_FIRST = (0, 1)
 ORDER = (
-    "z0", "t0", "x0", "t1", "z1", "t2", "x1", "t3", "z2", "m0", "x2", "t4", "z3", "x3",
-    "m1", "a0", "m2", "b0", "m3", "a1", "b1", "a2", "b2", "a3", "b3",
+    "t0", "t1", "z0", "t2", "x0", "z1", "t3", "x1", "z2", "m0", "t4", "x2", "z3", "x3",
+    "m1", "a0", "b0", "m2", "m3", "a1", "b1", "a2", "b2", "a3", "b3",
 )
 COLS = 256
 

time: 47.4 us -> 47.4 us (level)
  no operation moved by 1% of the time
where the time goes in v4:
time: 47.4 us; the launch traced here: 47.3 us
  Pallas kernels  45.4 us (96%)
  between operations  1.93 us (4%)
    pallas_call x1, Pallas kernels, shards(): pl.pallas_call(functools.partial(kernel, tiles, groups), out_shape=(pltpu...  44.2 us
    pallas_call x1, Pallas kernels, shards(): pl.pallas_call(write, out_shape=tuple((jax.ShapeDtypeStruct(x.shape, x.dt...  1.15 us

profile of v4, /device:TPU:1, one launch (start us, length us, event | category | flops | bytes accessed | tf_op | source)
XLA Modules:
  0.0 47.3 jit_solution(15516084694720843236)
XLA Ops:
  1.9 44.2 %shard_map.95 = (f32[2,32,128]{2,1,0:T(8,128)S(1)}, f32[10,32,1024]{2,1,0:T(8,128)S(1)}) custom-call(f32[10,32,1024]{2,1,0:T(8,128)} %coeffs.1, bf16[2,10,32,1024]{3,2,1,0:T(8,128)(2,1)} %perturb.1, bf16[1,5,1024,1024]{3,2,1,0:T(8,128)(2,1)} %blocks.1, s32[1,5]{1,0:T(1,128)} %neighbours_in.1, s32[1]{0:T(128)S(6)} %copy.10.live_in, s32[1]{0:T(128)S(6)} %copy.11.count_in, ...), custom_call_target="tpu_custom_call" | custom-call | flops 6710886400 | bytes 16777216 | tf_op jit(solution)/shard_map/pallas_call | solution.py:286
  46.1 1.1 %shard_map.96 = (f32[2,32,128]{2,1,0:T(8,128)}, f32[10,32,1024]{2,1,0:T(8,128)}) custom-call(f32[2,32,128]{2,1,0:T(8,128)S(1)} %get-tuple-element.4.inc, f32[10,32,1024]{2,1,0:T(8,128)S(1)} %get-tuple-element.5.grad), custom_call_target="tpu_custom_call" | custom-call | tf_op jit(solution)/shard_map/pallas_call | solution.py:337
